TPU v7x, 128 devices: a whole 4x4x4 slice. The times are simulated.
128 devices in a mesh: ep: 16 (over x, z), tp: 8 (over y, core).
Axes of the slice: x: 4, y: 4, z: 4, core: 2. Of those that a mesh axis runs over, the one named last changes fastest.
Arguments:
- tokens: bfloat16 [2, 2048, 4096], P(None, 'ep', 'tp'), may hold values from -6 to 6
- expert_ids: int32 [2, 2048, 8], P(None, 'ep'), may hold values from 0 to 63, all different within a row; in each aligned block of 128 rows (0 to 127, 128 to 255, ..., all dimensions but the last counted through in order) at most 20 rows name the same one
- route_weight: float32 [2, 2048, 8], P(None, 'ep'), may hold values from 0.1 to 1
- gate_weight: bfloat16 [64, 1536, 4096], P('ep', 'tp'), may hold values from -0.09375 to 0.09375
- up_weight: bfloat16 [64, 1536, 4096], P('ep', 'tp'), may hold values from -0.09375 to 0.09375
- down_weight: bfloat16 [64, 1536, 4096], P('ep', None, 'tp'), may hold values from -0.15625 to 0.15625
- home_slot: int32 [64], replicated, may hold values from 0 to 63, as said below
- spare_expert: int32 [16], replicated, may hold values from 0 to 63, as said below
Outputs:
- mixed: bfloat16 [2, 2048, 4096], P(None, 'ep', 'tp')
- spare_gate: bfloat16 [16, 1536, 4096], P('ep', 'tp')
- spare_up: bfloat16 [16, 1536, 4096], P('ep', 'tp')
- spare_down: bfloat16 [16, 1536, 4096], P('ep', None, 'tp')
Inputs may be any that keep to these rules, and one draw needn't show every extreme that they name: `home_slot`: a permutation; slot s belongs to ep index s // 4. `spare_expert`: names at most 6 distinct experts, whose home slots lie on distinct ep indices; entry d never names an expert whose home slot lies on ep index d. `expert_ids`: each token names 8 distinct experts; in each micro-step the 128 tokens of one ep index name one expert at most 20 times.
All inputs are finite; a program needn't handle non-finite values.
Results may differ from a plain program's by a relative error of at most 0.0058.
Values may be sent and summed in bfloat16 or wider, within the bound.
A program may use at most 192 MiB of HBM per device.

v0:
```python
import jax
import jax.numpy as jnp
from jax import lax
from jax.sharding import PartitionSpec as P

TOP = 8
STEPS = 2


def slot_targets(expert_pick, home_slot, capacity):
    count_all = home_slot.shape[0]
    expert_iota = lax.iota(jnp.int32, count_all)
    slot_pick = jnp.sum(jnp.where(expert_pick[..., None] == expert_iota, home_slot, 0), axis=-1)
    pair_shape = expert_pick.shape[:-2] + (expert_pick.shape[-2] * expert_pick.shape[-1],)
    pair_slot = slot_pick.reshape(pair_shape)
    one_hot = (pair_slot[..., None] == expert_iota).astype(jnp.int32)
    earlier = jnp.cumsum(one_hot, axis=-2) - one_hot
    position = jnp.sum(earlier * one_hot, axis=-1)
    return (pair_slot * capacity + position).reshape(expert_pick.shape)


def run_steps(tokens, expert_pick, route_weight, gate_weight, up_weight, down_weight, home_slot):
    batches = tokens.shape[0]
    tok_count = tokens.shape[1]
    width_local = tokens.shape[2]
    experts_all = home_slot.shape[0]
    local_count = gate_weight.shape[0]
    owners = experts_all // local_count
    capacity = tok_count * TOP * 5 // (4 * experts_all)
    slot_rows = local_count * capacity
    total_rows = experts_all * capacity
    own_target = slot_targets(expert_pick, home_slot, capacity)
    placing = jnp.any(own_target[..., None] == lax.iota(jnp.int32, total_rows), axis=2).astype(
        jnp.bfloat16
    )
    outgoing = jnp.einsum(
        "btr,btd->brd", placing, tokens, preferred_element_type=jnp.float32
    ).astype(jnp.bfloat16)
    outgoing = outgoing.reshape(batches, owners, slot_rows, width_local)
    arrived = lax.all_to_all(outgoing, "ep", split_axis=1, concat_axis=1, tiled=True)
    piece = lax.all_gather(arrived, "tp", axis=3, tiled=True)
    piece_rows = piece.reshape(batches, owners, local_count, capacity, piece.shape[3])
    gate_add = jnp.einsum(
        "bsecd,efd->bsecf", piece_rows, gate_weight, preferred_element_type=jnp.float32
    )
    up_add = jnp.einsum(
        "bsecd,efd->bsecf", piece_rows, up_weight, preferred_element_type=jnp.float32
    )
    hidden = (jax.nn.silu(gate_add) * up_add).astype(jnp.bfloat16)
    results = jnp.einsum(
        "bsecf,efd->bsecd",
        lax.all_gather(hidden, "tp", axis=4, tiled=True),
        down_weight,
        preferred_element_type=jnp.float32,
    ).astype(jnp.bfloat16)
    results = results.reshape(batches, owners, slot_rows, width_local)
    returned = lax.all_to_all(results, "ep", split_axis=1, concat_axis=1, tiled=True)
    returned = returned.reshape(batches, total_rows, width_local)
    flat_target = own_target.reshape(batches, tok_count * own_target.shape[2])
    picked_rows = jnp.take_along_axis(returned, flat_target[..., None], axis=1)
    picked_rows = picked_rows.reshape(batches, tok_count, own_target.shape[2], width_local).astype(
        jnp.float32
    )
    mixed = jnp.sum(picked_rows * route_weight[..., None], axis=2)
    return mixed.astype(jnp.bfloat16)


def move_spares(gate_weight, up_weight, down_weight, home_slot, spare_expert):
    local_count = gate_weight.shape[0]
    experts_all = home_slot.shape[0]
    owners = spare_expert.shape[0]
    own_index = lax.axis_index("ep")
    expert_iota = lax.iota(jnp.int32, experts_all)
    spare_slot = jnp.sum(jnp.where(spare_expert[:, None] == expert_iota, home_slot, 0), axis=1)
    spare_home = spare_slot // local_count
    own_slot = jnp.max(jnp.where(spare_home == own_index, spare_slot % local_count, 0))
    gate_part = lax.dynamic_index_in_dim(gate_weight, own_slot, 0, keepdims=False)
    up_part = lax.dynamic_index_in_dim(up_weight, own_slot, 0, keepdims=False)
    down_part = lax.dynamic_index_in_dim(down_weight, own_slot, 0, keepdims=False)
    gate_pieces = gate_part.reshape(gate_part.shape[0], owners, gate_part.shape[1] // owners)
    up_pieces = up_part.reshape(up_part.shape[0], owners, up_part.shape[1] // owners)
    down_pieces = down_part.reshape(down_part.shape[0], owners, down_part.shape[1] // owners)
    spread_gate, spread_up, spread_down = (
        lax.all_to_all(gate_pieces, "ep", split_axis=1, concat_axis=1, tiled=True),
        lax.all_to_all(up_pieces, "ep", split_axis=1, concat_axis=1, tiled=True),
        lax.all_to_all(down_pieces, "ep", split_axis=1, concat_axis=1, tiled=True),
    )
    chosen_gate = jnp.take(spread_gate, spare_home, axis=1)
    chosen_up = jnp.take(spread_up, spare_home, axis=1)
    chosen_down = jnp.take(spread_down, spare_home, axis=1)
    landed_gate, landed_up, landed_down = (
        lax.all_to_all(chosen_gate, "ep", split_axis=1, concat_axis=1, tiled=True),
        lax.all_to_all(chosen_up, "ep", split_axis=1, concat_axis=1, tiled=True),
        lax.all_to_all(chosen_down, "ep", split_axis=1, concat_axis=1, tiled=True),
    )
    spare_gate = landed_gate.reshape(1, gate_part.shape[0], gate_part.shape[1])
    spare_up = landed_up.reshape(1, up_part.shape[0], up_part.shape[1])
    spare_down = landed_down.reshape(1, down_part.shape[0], down_part.shape[1])
    return (spare_gate, spare_up, spare_down)


def shards(
    tokens, expert_ids, route_weight, gate_weight, up_weight, down_weight, home_slot, spare_expert
):
    spare_gate, spare_up, spare_down = move_spares(
        gate_weight, up_weight, down_weight, home_slot, spare_expert
    )
    outputs = [
        run_steps(
            tokens[step_index : step_index + 1],
            expert_ids[step_index : step_index + 1],
            route_weight[step_index : step_index + 1],
            gate_weight,
            up_weight,
            down_weight,
            home_slot,
        )
        for step_index in range(STEPS)
    ]
    mixed = jnp.concatenate(outputs, axis=0)
    return (mixed, spare_gate, spare_up, spare_down)


def solution(mesh):
    placed = (
        P(None, "ep", "tp"),
        P(None, "ep", None),
        P(None, "ep", None),
        P("ep", "tp", None),
        P("ep", "tp", None),
        P("ep", None, "tp"),
        P(),
        P(),
    )
    return jax.shard_map(
        shards,
        mesh=mesh,
        in_specs=placed,
        out_specs=(
            P(None, "ep", "tp"),
            P("ep", "tp", None),
            P("ep", "tp", None),
            P("ep", None, "tp"),
        ),
        check_vma=False,
    )
```

profile of v0, /device:TPU:1, one launch (start us, length us, event | category | flops | bytes accessed | tf_op | source)
XLA Modules:
  0.0 523.6 jit_solution(15135955831022527040)
XLA Ops:
  7.2 0.7 slice_bitcast_fusion.3
  7.9 0.8 select_reduce_fusion.1
  9.0 18.0 %reduce-window.14 = s32[1,64,8,128]{3,2,1,0:T(8,128)S(1)} reduce-window(s32[1,64,8,128]{3,2,1,0:T(8,128)S(1)} %bitcast.226, s32[]{:T(128)} %constant.82.clone.1), window={size=1x1x1x128 pad=0_0x0_0x0_0x127_0}, to_apply=%region_1.2 | reduce-window | flops 8323072 | bytes 524292 | tf_op jit(solution)/shard_map/reduce-window
  27.5 18.0 %reduce-window.16 = s32[1,64,8,128]{3,2,1,0:T(8,128)S(1)} reduce-window(s32[1,64,8,128]{3,2,1,0:T(8,128)S(1)} %bitcast.227, s32[]{:T(128)} %constant.82.clone.1), window={size=1x1x1x128 pad=0_0x0_0x0_0x127_0}, to_apply=%region_7.9 | reduce-window | flops 8323072 | bytes 524292 | tf_op jit(solution)/shard_map/reduce-window.2
  47.2 1.6 fusion.12
  48.9 0.6 convolution_convert_fusion.1
  49.4 27.1 %all_to_all.50 = bf16[1,16,80,512]{3,2,0,1:T(8,128)(2,1)S(1)} all-to-all(bf16[1,16,80,512]{3,2,0,1:T(8,128)(2,1)S(1)} %bitcast.222), channel_id=1, replica_groups=mesh['ep'=16,'tp'=8] {'ep'}, dimensions={1} | all-to-all | bytes 2621440 | tf_op jit(solution)/shard_map/all_to_all | solution.py:40
  76.6 1.8 copy.91
  78.5 1.6 fusion.13
  80.1 0.6 convolution_convert_fusion
  80.7 20.5 %all_to_all.51 = bf16[1,16,80,512]{3,2,0,1:T(8,128)(2,1)S(1)} all-to-all(bf16[1,16,80,512]{3,2,0,1:T(8,128)(2,1)S(1)} %bitcast.223), channel_id=1, replica_groups=mesh['ep'=16,'tp'=8] {'ep'}, dimensions={1} | all-to-all | bytes 2621440 | tf_op jit(solution)/shard_map/all_to_all | solution.py:40
  101.2 1.8 copy.104
  103.2 33.6 %all-gather.5.cloned.1.call-done = bf16[1,16,80,4096]{3,1,2,0:T(8,128)(2,1)} async-done(((bf16[1,16,80,512]{3,1,2,0:T(8,128)(2,1)}), bf16[1,16,80,4096]{3,1,2,0:T(8,128)(2,1)}) %all-gather.5.cloned.1.call-update) | async-done | bytes 10485776 | tf_op jit(solution)/shard_map/all_gather | solution.py:41
  136.8 8.8 %fusion.38 = f32[1,16,4,20,192]{4,1,3,2,0:T(8,128)S(1)} fusion(bf16[16,4,20,4096]{3,0,2,1:T(8,128)(2,1)} %bitcast.238, bf16[4,192,4096]{2,1,0:T(8,128)(2,1)} %param.15), kind=kOutput, calls=%fused_computation.36 | convolution fusion | flops 2013265920 | bytes 17760256 | tf_op jit(solution)/shard_map/bsecd,efd->bsecf/dot_general | solution.py:43
  145.6 10.5 %fusion.59 = bf16[1,16,4,20,192]{4,1,3,2,0:T(8,128)(2,1)S(1)} fusion(bf16[16,4,20,4096]{3,0,2,1:T(8,128)(2,1)} %bitcast.239, bf16[4,192,4096]{2,1,0:T(8,128)(2,1)} %param.16, f32[1,16,4,20,192]{4,1,3,2,0:T(8,128)S(1)} %fusion.38), kind=kOutput, calls=%fused_computation.43 | convolution fusion | flops 2014740480 | bytes 18251776 | tf_op jit(solution)/shard_map/bsecd,efd->bsecf/dot_general | solution.py:46
  156.1 4.1 copy.92
  160.2 0.6 copy-done.6
  161.1 0.6 compare_select_fusion.2
  163.7 2.3 constant_dynamic-slice_fusion
  166.0 0.4 copy.122
  166.4 1.7 copy.110
  168.1 6.4 %all-to-all-start.4 = ((bf16[192,16,256]{2,0,1:T(8,128)(2,1)}), bf16[192,16,256]{2,0,1:T(8,128)(2,1)S(1)}, u32[]{:S(2)}, u32[]{:S(2)}) async-start(bf16[192,16,256]{2,0,1:T(8,128)(2,1)} %copy.110), calls=%async_computation.4 | async-start | bytes 3145728 | tf_op jit(solution)/shard_map/all_to_all | solution.py:84
  175.0 1.7 copy.112
  176.7 21.2 %all-gather.9.cloned.1.call-done = bf16[1,16,80,4096]{3,1,2,0:T(8,128)(2,1)} async-done(((bf16[1,16,80,512]{3,1,2,0:T(8,128)(2,1)}), bf16[1,16,80,4096]{3,1,2,0:T(8,128)(2,1)}) %all-gather.9.cloned.1.call-update) | async-done | bytes 10485776 | tf_op jit(solution)/shard_map/all_gather | solution.py:41
  197.9 9.7 %fusion.41 = f32[1,16,4,20,192]{4,1,3,2,0:T(8,128)} fusion(bf16[16,4,20,4096]{3,0,2,1:T(8,128)(2,1)} %bitcast.236, bf16[4,192,4096]{2,1,0:T(8,128)(2,1)} %param.15), kind=kOutput, calls=%fused_computation.37 | convolution fusion | flops 2013265920 | bytes 17760256 | tf_op jit(solution)/shard_map/bsecd,efd->bsecf/dot_general | solution.py:43
  207.6 6.7 %all-to-all-start.6 = ((bf16[192,16,256]{2,0,1:T(8,128)(2,1)}), bf16[192,16,256]{2,0,1:T(8,128)(2,1)S(1)}, u32[]{:S(2)}, u32[]{:S(2)}) async-start(bf16[192,16,256]{2,0,1:T(8,128)(2,1)} %copy.112), calls=%async_computation.6 | async-start | bytes 3145728 | tf_op jit(solution)/shard_map/all_to_all | solution.py:85
  214.6 11.5 %fusion.56 = bf16[1,16,4,20,192]{4,1,3,2,0:T(8,128)(2,1)} fusion(bf16[16,4,20,4096]{3,0,2,1:T(8,128)(2,1)} %bitcast.237, bf16[4,192,4096]{2,1,0:T(8,128)(2,1)} %param.16, f32[1,16,4,20,192]{4,1,3,2,0:T(8,128)} %fusion.41), kind=kOutput, calls=%fused_computation.42 | convolution fusion | flops 2014740480 | bytes 18251776 | tf_op jit(solution)/shard_map/bsecd,efd->bsecf/dot_general | solution.py:46
  226.1 5.3 %copy.105 = bf16[1,16,4,20,192]{3,1,2,0,4:T(8,128)(2,1)} copy(bf16[1,16,4,20,192]{4,1,3,2,0:T(8,128)(2,1)} %fusion.56) | data formatting | bytes 983040 | tf_op jit(solution)/shard_map/convert_element_type | solution.py:49
  231.4 2.7 constant_dynamic-slice_fusion.2
  234.1 2.7 copy.119
  236.8 0.5 all-to-all-done.6
  237.3 1.1 copy-done.1
  238.4 6.4 %all-to-all-start.8 = ((bf16[1536,16,32]{0,2,1:T(8,128)(2,1)}), bf16[1536,16,32]{0,2,1:T(8,128)(2,1)S(1)}, u32[]{:S(2)}, u32[]{:S(2)}) async-start(bf16[1536,16,32]{0,2,1:T(8,128)(2,1)} %bitcast.71), calls=%async_computation.8 | async-start | bytes 3145728 | tf_op jit(solution)/shard_map/all_to_all | solution.py:86
  244.8 1.8 gather_fusion.3
  246.6 3.2 gather_fusion.4
  249.8 3.6 select_bitcast_fusion
  253.3 13.5 %all-to-all-done.8 = bf16[1536,16,32]{0,2,1:T(8,128)(2,1)S(1)} async-done(((bf16[1536,16,32]{0,2,1:T(8,128)(2,1)}), bf16[1536,16,32]{0,2,1:T(8,128)(2,1)S(1)}, u32[]{:S(2)}, u32[]{:S(2)}) %all-to-all-start.8) | async-done | bytes 1572896 | tf_op jit(solution)/shard_map/all_to_all | solution.py:86
  266.8 24.6 %all_to_all.52 = bf16[192,16,256]{2,0,1:T(8,128)(2,1)} all-to-all(bf16[192,16,256]{2,0,1:T(8,128)(2,1)S(1)} %get-tuple-element.39), channel_id=1, replica_groups=mesh['ep'=16,'tp'=8] {'ep'}, dimensions={1} | all-to-all | bytes 3145728 | tf_op jit(solution)/shard_map/all_to_all | solution.py:92
  291.5 4.4 all-to-all-start.7
  295.9 0.6 gather_fusion
  296.6 1.4 select_bitcast_fusion.2
  297.9 17.9 %all-to-all-done.7 = bf16[192,16,256]{2,0,1:T(8,128)(2,1)} async-done(((bf16[192,16,256]{2,0,1:T(8,128)(2,1)}), bf16[192,16,256]{2,0,1:T(8,128)(2,1)}, u32[]{:S(2)}, u32[]{:S(2)}) %all-to-all-start.7) | async-done | bytes 1572896 | tf_op jit(solution)/shard_map/all_to_all | solution.py:93
  315.8 4.6 all-to-all-start.9
  320.4 27.8 %copy.93 = bf16[1,16,4,20,1536]{4,3,1,2,0:T(8,128)(2,1)} copy(bf16[1,16,4,20,1536]{3,1,2,0,4:T(8,128)(2,1)} %all-gather.7.cloned.1.call-done) | data formatting | bytes 7864320 | tf_op jit(solution)/shard_map/all_gather | solution.py:52
  348.3 7.2 %fusion.33 = bf16[1,16,4,20,512]{4,3,1,2,0:T(8,128)(2,1)S(1)} fusion(bf16[4,1536,512]{2,1,0:T(8,128)(2,1)} %param.17, bf16[1,16,4,20,1536]{4,3,1,2,0:T(8,128)(2,1)} %copy.93), kind=kOutput, calls=%fused_computation.35 | convolution fusion | flops 2013921280 | bytes 11534336 | tf_op jit(solution)/shard_map/bsecf,efd->bsecd/dot_general | solution.py:50
  355.9 1.8 copy.95
  357.7 1.2 copy-done
  358.8 7.0 %all-to-all-start.1 = ((bf16[1,16,80,512]{3,2,0,1:T(8,128)(2,1)}), bf16[1,16,80,512]{3,2,0,1:T(8,128)(2,1)S(1)}, u32[]{:S(2)}, u32[]{:S(2)}) async-start(bf16[1,16,80,512]{3,2,0,1:T(8,128)(2,1)} %copy.95), calls=%async_computation.1 | async-start | bytes 2621440 | tf_op jit(solution)/shard_map/all_to_all | solution.py:57
  365.9 77.1 %all-gather.11.cloned.1.call-done = bf16[1,16,4,20,1536]{3,1,2,0,4:T(8,128)(2,1)} async-done(((bf16[1,16,4,20,192]{3,1,2,0,4:T(8,128)(2,1)}), bf16[1,16,4,20,1536]{3,1,2,0,4:T(8,128)(2,1)}) %all-gather.11.cloned.1.call-update) | async-done | bytes 3932176 | tf_op jit(solution)/shard_map/all_gather | solution.py:52
  443.0 27.2 %copy.106 = bf16[1,16,4,20,1536]{4,3,1,2,0:T(8,128)(2,1)} copy(bf16[1,16,4,20,1536]{3,1,2,0,4:T(8,128)(2,1)} %all-gather.11.cloned.1.call-done) | data formatting | bytes 7864320 | tf_op jit(solution)/shard_map/all_gather | solution.py:52
  470.2 6.9 %fusion.28 = bf16[1,16,4,20,512]{4,3,1,2,0:T(8,128)(2,1)S(1)} fusion(bf16[4,1536,512]{2,1,0:T(8,128)(2,1)} %param.17, bf16[1,16,4,20,1536]{4,3,1,2,0:T(8,128)(2,1)} %copy.106), kind=kOutput, calls=%fused_computation.34 | convolution fusion | flops 2013921280 | bytes 11534336 | tf_op jit(solution)/shard_map/bsecf,efd->bsecd/dot_general | solution.py:50
  477.5 1.8 copy.108
  479.3 6.8 %all-to-all-start.3 = ((bf16[1,16,80,512]{3,2,0,1:T(8,128)(2,1)}), bf16[1,16,80,512]{3,2,0,1:T(8,128)(2,1)S(1)}, u32[]{:S(2)}, u32[]{:S(2)}) async-start(bf16[1,16,80,512]{3,2,0,1:T(8,128)(2,1)} %copy.108), calls=%async_computation.3 | async-start | bytes 2621440 | tf_op jit(solution)/shard_map/all_to_all | solution.py:57
  486.8 3.4 copy.111
  490.2 3.7 reshape.655
  494.0 3.4 copy.113
  497.4 3.7 reshape.657
  501.1 2.6 copy.115
  503.7 5.1 gather_fusion.1
  508.8 5.1 gather_fusion.2
  513.9 0.8 fusion.17
  514.6 0.4 copy-done.3
  515.1 0.8 fusion.16
  515.9 0.7 pad_maximum_fusion
  (77 shorter events, 5.2 us)
Async XLA Ops:
  7.2 129.7 %all-gather.5.cloned.1.call-start = ((), (), s32[]{:S(2)}) async-start(), calls=%async_computation.10 | async-start | bytes 11796480 | tf_op jit(solution)/shard_map/all_gather | solution.py:41
  46.1 2.7 copy-start.4
  78.4 119.6 %all-gather.9.cloned.1.call-start = ((), (), s32[]{:S(2)}) async-start(), calls=%async_computation.12 | async-start | bytes 11796480 | tf_op jit(solution)/shard_map/all_gather | solution.py:41
  103.0 217.4 %all-gather.7.cloned.1.call-start = ((), (), s32[]{:S(2)}) async-start(), calls=%async_computation.11 | async-start | bytes 28311552 | tf_op jit(solution)/shard_map/all_gather | solution.py:52
  160.2 0.7 copy-start.6
  160.2 0.7 copy-start.7
  168.1 39.5 %all-to-all-start.4 = ((bf16[192,16,256]{2,0,1:T(8,128)(2,1)}), bf16[192,16,256]{2,0,1:T(8,128)(2,1)S(1)}, u32[]{:S(2)}, u32[]{:S(2)}) async-start(bf16[192,16,256]{2,0,1:T(8,128)(2,1)} %copy.110), calls=%async_computation.4 | async-start | bytes 3145728 | tf_op jit(solution)/shard_map/all_to_all | solution.py:84
  207.6 29.6 %all-to-all-start.6 = ((bf16[192,16,256]{2,0,1:T(8,128)(2,1)}), bf16[192,16,256]{2,0,1:T(8,128)(2,1)S(1)}, u32[]{:S(2)}, u32[]{:S(2)}) async-start(bf16[192,16,256]{2,0,1:T(8,128)(2,1)} %copy.112), calls=%async_computation.6 | async-start | bytes 3145728 | tf_op jit(solution)/shard_map/all_to_all | solution.py:85
  214.3 228.7 %all-gather.11.cloned.1.call-start = ((), (), s32[]{:S(2)}) async-start(), calls=%async_computation.13 | async-start | bytes 28311552 | tf_op jit(solution)/shard_map/all_gather | solution.py:52
  237.3 1.1 copy-start.1
  238.4 28.4 %all-to-all-start.8 = ((bf16[1536,16,32]{0,2,1:T(8,128)(2,1)}), bf16[1536,16,32]{0,2,1:T(8,128)(2,1)S(1)}, u32[]{:S(2)}, u32[]{:S(2)}) async-start(bf16[1536,16,32]{0,2,1:T(8,128)(2,1)} %bitcast.71), calls=%async_computation.8 | async-start | bytes 3145728 | tf_op jit(solution)/shard_map/all_to_all | solution.py:86
  291.5 24.3 %all-to-all-start.7 = ((bf16[192,16,256]{2,0,1:T(8,128)(2,1)}), bf16[192,16,256]{2,0,1:T(8,128)(2,1)}, u32[]{:S(2)}, u32[]{:S(2)}) async-start(bf16[192,16,256]{2,0,1:T(8,128)(2,1)} %get-tuple-element.38), calls=%async_computation.7 | async-start | bytes 3145728 | tf_op jit(solution)/shard_map/all_to_all | solution.py:93
  315.8 41.9 %all-to-all-start.9 = ((bf16[1536,16,32]{0,2,1:T(8,128)(2,1)}), bf16[1536,16,32]{0,2,1:T(8,128)(2,1)S(1)}, u32[]{:S(2)}, u32[]{:S(2)}) async-start(bf16[1536,16,32]{0,2,1:T(8,128)(2,1)} %select_bitcast_fusion.2), calls=%async_computation.9 | async-start | bytes 3145728 | tf_op jit(solution)/shard_map/all_to_all | solution.py:94
  357.7 1.2 copy-start
  358.8 120.5 %all-to-all-start.1 = ((bf16[1,16,80,512]{3,2,0,1:T(8,128)(2,1)}), bf16[1,16,80,512]{3,2,0,1:T(8,128)(2,1)S(1)}, u32[]{:S(2)}, u32[]{:S(2)}) async-start(bf16[1,16,80,512]{3,2,0,1:T(8,128)(2,1)} %copy.95), calls=%async_computation.1 | async-start | bytes 2621440 | tf_op jit(solution)/shard_map/all_to_all | solution.py:57
  479.3 7.0 %copy-start.5 = (f32[2,128,8]{1,2,0:T(8,128)S(1)}, f32[2,128,8]{1,2,0:T(8,128)}, u32[]{:S(2)}) copy-start(f32[2,128,8]{1,2,0:T(8,128)} %param.14) | copy-start | bytes 24580
  479.3 29.5 %all-to-all-start.3 = ((bf16[1,16,80,512]{3,2,0,1:T(8,128)(2,1)}), bf16[1,16,80,512]{3,2,0,1:T(8,128)(2,1)S(1)}, u32[]{:S(2)}, u32[]{:S(2)}) async-start(bf16[1,16,80,512]{3,2,0,1:T(8,128)(2,1)} %copy.108), calls=%async_computation.3 | async-start | bytes 2621440 | tf_op jit(solution)/shard_map/all_to_all | solution.py:57
  508.8 5.1 copy-start.2
  513.9 1.2 copy-start.3
Sparse Core Ops, SparseCore 0:
  78.5 58.2 all-gather.4
  139.1 58.7 all-gather.8
  199.6 120.5 all-gather.6
  321.8 121.2 all-gather.10
where the time goes:
time: 532 us; the launch traced here: 524 us
  waiting for transfers between devices  164 us (31%)
  local copies, waits for them, and re-layouts  124 us (23%)
  blocking collectives  72.3 us (14%)
  matrix products  55.7 us (10%)
  other arithmetic  48.5 us (9%)
  starting transfers between devices  42.9 us (8%)
  between operations  16.6 us (3%)
    all_gather x2, waiting for transfers between devices, run_steps(): lax.all_gather(hidden, 'tp', axis=4, tiled=True)  77.2 us
    all_gather x2, local copies, waits for them, and re-layouts, run_steps(): lax.all_gather(hidden, 'tp', axis=4, tiled=True)  55 us
    all_gather x2, waiting for transfers between devices, run_steps(): piece = lax.all_gather(arrived, 'tp', axis=3, tiled=True)  54.8 us
    all_to_all x2, blocking collectives, run_steps(): lax.all_to_all(outgoing, 'ep', split_axis=1, concat_axis=1, tiled=True)  47.6 us
    another operation x4, other arithmetic  36.1 us
    all_to_all x1, blocking collectives, move_spares(): lax.all_to_all(chosen_gate, 'ep', split_axis=1, concat_axis=1, tiled=True)  24.6 us
    dot_general x2, matrix products, run_steps(): jnp.einsum('bsecd,efd->bsecf', piece_rows, up_weight, preferred_element_t...  22 us
    dot_general x2, matrix products, run_steps(): jnp.einsum('bsecd,efd->bsecf', piece_rows, gate_weight, preferred_element...  18.5 us
  transfers between devices with their start and end apart: 11, of which 6 were waited for; matrix products, arithmetic and copies ran while one was open for 33% of the time, Pallas kernels for 0%

commit v1 on v0

v1 whole, which is shorter than its diff:
```python
import functools

import jax
import jax.numpy as jnp
import numpy as np
from jax import lax
from jax.experimental import pallas as pl
from jax.experimental.pallas import tpu as pltpu
from jax.sharding import PartitionSpec as P

MESH = pl.DeviceIdType.MESH
BF16 = jnp.bfloat16
F32 = jnp.float32
STEPS = 2
SIDE = 4
CAP = 20
SLOTS = 64
TOK = 128
BLOCK = 4 * CAP
ROWS = 16 * CAP
PIECE = 288
ANY = pl.BlockSpec(memory_space=pl.ANY)
VM = pl.BlockSpec(memory_space=pltpu.VMEM)
SM = pl.BlockSpec(memory_space=pltpu.SMEM)


def dot(a, b):
    return jnp.dot(a, b, preferred_element_type=F32)


def dot_t(a, b):
    return lax.dot_general(a, b, (((1,), (1,)), ((), ())), preferred_element_type=F32)


def iota(shape, dim):
    return lax.broadcasted_iota(jnp.int32, shape, dim)


def pack_kernel(own_ref, ids_ref, home_ref, tok_ref, wg, wu, wd, out_ref, pieces, sem):
    own = own_ref[0]

    def copies(j):
        h, p = j // 16, lax.rem(j, 16)
        px, pz = p // 4, lax.rem(p, 4)
        columns = pl.ds(pl.multiple_of(p * 256, 256), 256)
        rows = pl.ds(pl.multiple_of(h * 96, 16), 96)
        low = pl.ds(pl.multiple_of(h * 768 + p * 48, 16), 48)
        to = pieces.at[h, px, pz]
        return [
            pltpu.make_async_copy(wg.at[own, rows, columns], to.at[pl.ds(0, 96)], sem.at[j, 0]),
            pltpu.make_async_copy(wu.at[own, rows, columns], to.at[pl.ds(96, 96)], sem.at[j, 1]),
            pltpu.make_async_copy(wd.at[own, low, pl.ds(0, 256)], to.at[pl.ds(192, 48)], sem.at[j, 2]),
            pltpu.make_async_copy(wd.at[own, low, pl.ds(256, 256)], to.at[pl.ds(240, 48)], sem.at[j, 3]),
        ]

    def start(j, _):
        for c in copies(j):
            c.start()
        return 0

    lax.fori_loop(0, 32, start, 0)
    perm = (home_ref[...] == iota((SLOTS, SLOTS), 0)).astype(BF16)
    before = (iota((TOK, TOK), 0) < iota((TOK, TOK), 1)).astype(BF16)
    for s in range(STEPS):
        named = iota((SLOTS, TOK), 0)
        picked = jnp.zeros((SLOTS, TOK), F32)
        for k in range(8):
            picked = jnp.where(ids_ref[s, k : k + 1, :] == named, 1.0, picked)
        by_slot = dot(perm, picked.astype(BF16))
        position = dot(by_slot.astype(BF16), before)
        value = jnp.where(by_slot > 0.5, position, -1.0).astype(BF16)
        for x in range(SIDE):
            row = iota((ROWS, SLOTS), 0) + x * ROWS
            low = iota((ROWS, SLOTS), 1) * CAP
            spread = jnp.where((row >= low) & (row < low + CAP), 1.0, 0.0).astype(BF16)
            row = iota((ROWS, TOK), 0) + x * ROWS
            within = (row - ((row * 3277) >> 16) * CAP).astype(F32)
            placing = jnp.where(dot(spread, value) == within, 1.0, 0.0).astype(BF16)
            for h in range(2):
                block = dot(placing, tok_ref[s, :, h * 256 : (h + 1) * 256]).astype(BF16)
                out_ref[s, h, x] = block.reshape(SIDE, BLOCK, 256)

    def finish(j, _):
        for c in copies(j):
            c.wait()
        return 0

    lax.fori_loop(0, 32, finish, 0)


def mix_kernel(ids_ref, rw_ref, home_ref, back_ref, pieces, mixed_ref, gate, up, down, sem):
    def copies(j):
        h, p = j // 16, lax.rem(j, 16)
        px, pz = p // 4, lax.rem(p, 4)
        columns = pl.ds(pl.multiple_of(p * 256, 256), 256)
        rows = pl.ds(pl.multiple_of(h * 96, 16), 96)
        low = pl.ds(pl.multiple_of(h * 768 + p * 48, 16), 48)
        of = pieces.at[h, px, pz]
        return [
            pltpu.make_async_copy(of.at[pl.ds(0, 96)], gate.at[0, rows, columns], sem.at[j, 0]),
            pltpu.make_async_copy(of.at[pl.ds(96, 96)], up.at[0, rows, columns], sem.at[j, 1]),
            pltpu.make_async_copy(of.at[pl.ds(192, 48)], down.at[0, low, pl.ds(0, 256)], sem.at[j, 2]),
            pltpu.make_async_copy(of.at[pl.ds(240, 48)], down.at[0, low, pl.ds(256, 256)], sem.at[j, 3]),
        ]

    def start(j, _):
        for c in copies(j):
            c.start()
        return 0

    lax.fori_loop(0, 32, start, 0)
    perm = (home_ref[...] == iota((SLOTS, SLOTS), 1)).astype(BF16)
    before = (iota((TOK, TOK), 1) < iota((TOK, TOK), 0)).astype(BF16)
    for s in range(STEPS):
        named = iota((TOK, SLOTS), 1)
        picked = jnp.zeros((TOK, SLOTS), F32)
        scale = jnp.zeros((TOK, SLOTS), F32)
        for k in range(8):
            match = ids_ref[s, :, k : k + 1] == named
            picked = jnp.where(match, 1.0, picked)
            scale = jnp.where(match, rw_ref[s, :, k : k + 1], scale)
        by_slot = dot(picked.astype(BF16), perm)
        position = dot(before, by_slot.astype(BF16))
        value = jnp.where(by_slot > 0.5, position, -1.0).astype(BF16)
        high = scale.astype(BF16)
        rest = (scale - high.astype(F32)).astype(BF16)
        high = dot(high, perm).astype(BF16)
        rest = dot(rest, perm).astype(BF16)
        totals = [jnp.zeros((TOK, 256), F32)] * 2
        for x in range(SIDE):
            row = iota((SLOTS, ROWS), 1) + x * ROWS
            low = iota((SLOTS, ROWS), 0) * CAP
            spread = jnp.where((row >= low) & (row < low + CAP), 1.0, 0.0).astype(BF16)
            row = iota((TOK, ROWS), 1) + x * ROWS
            within = (row - ((row * 3277) >> 16) * CAP).astype(F32)
            here = dot(value, spread) == within
            high_row = jnp.where(here, dot(high, spread), 0.0).astype(BF16)
            rest_row = jnp.where(here, dot(rest, spread), 0.0).astype(BF16)
            for h in range(2):
                block = back_ref[s, h, x].reshape(ROWS, 256)
                totals[h] = totals[h] + dot(high_row, block) + dot(rest_row, block)
        for h in range(2):
            mixed_ref[s, :, h * 256 : (h + 1) * 256] = totals[h].astype(BF16)

    def finish(j, _):
        for c in copies(j):
            c.wait()
        return 0

    lax.fori_loop(0, 32, finish, 0)


class Exchange:
    def __init__(self, number, src, mid, dst, send, recv):
        ep, tp = lax.axis_index("ep"), lax.axis_index("tp")
        self.ex, self.ez, self.tp = ep // SIDE, lax.rem(ep, SIDE), tp
        self.src, self.mid, self.dst = src, mid, dst
        self.send, self.recv, self.number = send, recv, number
        self.started = []

    def copy(self, phase, half, d):
        ex, ez = self.ex, self.ez
        along_x = half == phase
        x = lax.rem(ex + d, SIDE) if along_x else ex
        z = ez if along_x else lax.rem(ez + d, SIDE)
        if phase == 0:
            a = self.src.at[0, x] if half == 0 else self.src.at[1, :, z]
            b = self.mid.at[half, ex if half == 0 else ez]
        else:
            a = self.mid.at[half, :, z if half == 0 else x]
            b = self.dst.at[0, :, ez] if half == 0 else self.dst.at[1, ex]
        send = self.send.at[self.number, phase, half, d]
        if d == 0:
            return pltpu.make_async_copy(a, b, send)
        recv = self.recv.at[self.number, phase, half, d]
        return pltpu.make_async_remote_copy(
            a, b, send, recv, device_id=(x * SIDE + z, self.tp), device_id_type=MESH
        )

    def start(self, phase):
        for d in (2, 1, 3, 0):
            for half in range(2):
                c = self.copy(phase, half, d)
                c.start()
                self.started.append((phase, d, c))

    def arrive(self, phase):
        for at, d, c in self.started:
            if at == phase:
                c.wait() if d == 0 else c.wait_recv()

    def forward(self):
        self.arrive(0)
        self.start(1)

    def sent(self):
        for _, d, c in self.started:
            if d:
                c.wait_send()


class Ring:
    def __init__(self, number, ref, width, send, recv):
        self.ep, self.tp = lax.axis_index("ep"), lax.axis_index("tp")
        self.y = self.tp // 2
        self.ref, self.width, self.number = ref, width, number
        self.send, self.recv = send, recv
        self.all = {}

    def copy(self, kind):
        y = lax.rem(self.y + (0, 0, 3, 1)[kind], 4)
        to = lax.rem(self.tp + (2, 6, 2, 6)[kind], 8)
        rows = (pl.ds(0, ROWS), pl.ds(0, ROWS), pl.ds(0, ROWS // 2), pl.ds(ROWS // 2, ROWS // 2))[kind]
        part = self.ref.at[rows, pl.ds(pl.multiple_of(y * self.width, 128), self.width)]
        return pltpu.make_async_remote_copy(
            part,
            part,
            self.send.at[self.number, kind],
            self.recv.at[self.number, kind],
            device_id=(self.ep, to),
            device_id_type=MESH,
        )

    def start(self):
        for kind in (0, 1):
            self.all[kind] = self.copy(kind)
            self.all[kind].start()

    def forward(self):
        for kind in (0, 1):
            self.all[kind].wait_recv()
            self.all[kind + 2] = self.copy(kind + 2)
            self.all[kind + 2].start()

    def arrive(self):
        for kind in (2, 3):
            self.all[kind].wait_recv()

    def sent(self):
        for c in self.all.values():
            c.wait_send()


def main_kernel(
    sel, perm, outgoing, pieces, wg, wu, wd,
    returned, landed, mid_a, mid_b, mid_r,
    gate_w, up_w, down_w, xs, hs, swap, outs, arrived, results, mid_d, spread, chosen, acc,
    a_send, a_recv, x_send, x_recv, h_send, h_recv, c_send, c_recv, w_send, w_recv, w_local,
):
    ep, tp = lax.axis_index("ep"), lax.axis_index("tp")
    ex, ez = ep // SIDE, lax.rem(ep, SIDE)
    core = lax.rem(tp, 2)
    mate = (ep, tp + 1 - 2 * core)

    barrier = pltpu.get_barrier_semaphore()
    for d in range(1, SIDE):
        pl.semaphore_signal(barrier, inc=1, device_id=(lax.rem(ex + d, SIDE) * SIDE + ez, tp), device_id_type=MESH)
        pl.semaphore_signal(barrier, inc=1, device_id=(ex * SIDE + lax.rem(ez + d, SIDE), tp), device_id_type=MESH)
    pl.semaphore_signal(barrier, inc=1, device_id=(ep, lax.rem(tp + 2, 8)), device_id_type=MESH)
    pl.semaphore_signal(barrier, inc=1, device_id=(ep, lax.rem(tp + 6, 8)), device_id_type=MESH)
    pl.semaphore_signal(barrier, inc=1, device_id=mate, device_id_type=MESH)
    pl.semaphore_wait(barrier, 9)

    deal = [Exchange(s, outgoing.at[s], mid_d.at[s], arrived.at[s], a_send, a_recv) for s in range(STEPS)]
    give = [Exchange(2 + s, results.at[s], mid_r.at[s], returned.at[s], a_send, a_recv) for s in range(STEPS)]
    scatter = Exchange(4, pieces, mid_a, spread, a_send, a_recv)
    gather = Exchange(5, chosen, mid_b, landed, a_send, a_recv)
    x_ring = [Ring(q, xs.at[q // 2, q % 2], 1024, x_send, x_recv) for q in range(4)]
    h_ring = [Ring(q, hs.at[q // 2, q % 2], 384, h_send, h_recv) for q in range(4)]

    deal[0].start(0)
    deal[1].start(0)

    own_two, mate_two = pl.ds(2 * core, 2), pl.ds(2 - 2 * core, 2)
    own_rows = pl.ds(pl.multiple_of(core * 192, 16), 192)
    own_half = pl.ds(pl.multiple_of(core * 512, 512), 512)
    mate_half = pl.ds(pl.multiple_of(512 - core * 512, 512), 512)
    weights = []
    for n, (w, held) in enumerate(((wg, gate_w), (wu, up_w), (wd, down_w))):
        to = held.at[:, :, own_half] if n == 2 else held.at[:, own_rows]
        mine = pltpu.make_async_copy(w.at[own_two], to, w_local.at[n])
        theirs = pltpu.make_async_remote_copy(
            w.at[mate_two], to, w_send.at[n], w_recv.at[n], device_id=mate, device_id_type=MESH
        )
        mine.start()
        theirs.start()
        weights.append((mine, theirs))

    own_perm = pl.ds(pl.multiple_of(core * 160, 16), 160)
    mate_perm = pl.ds(pl.multiple_of(160 - core * 160, 16), 160)

    def regroup(s):
        def one(g, _):
            rows = pl.ds(pl.multiple_of(g * BLOCK, 16), BLOCK)
            for h in range(2):
                block = arrived[s, h, g].reshape(ROWS, 256)
                mine = dot(perm[own_perm, :], block).astype(BF16)
                theirs = dot(perm[mate_perm, :], block).astype(BF16)
                columns = pl.ds(pl.multiple_of(tp * 512 + h * 256, 256), 256)
                for i in range(2):
                    xs[s, i, rows, columns] = mine[i * BLOCK : (i + 1) * BLOCK]
                    swap[s, i, rows, pl.ds(h * 256, 256)] = theirs[i * BLOCK : (i + 1) * BLOCK]
            return 0

        lax.fori_loop(0, SIDE, one, 0)
        c = pltpu.make_async_remote_copy(
            swap.at[s],
            xs.at[s, :, :, pl.ds(pl.multiple_of(tp * 512, 512), 512)],
            c_send.at[s],
            c_recv.at[s],
            device_id=mate,
            device_id_type=MESH,
        )
        c.start()
        return c

    def hidden(q):
        s, i = q // 2, q % 2
        acc[...] = jnp.zeros_like(acc)

        def one(k, _):
            columns = pl.ds(pl.multiple_of(k * 512, 512), 512)
            block = xs[s, i, :, columns]
            acc[0] += dot_t(block, gate_w[i, :, columns])
            acc[1] += dot_t(block, up_w[i, :, columns])
            return 0

        lax.fori_loop(0, 8, one, 0)
        columns = pl.ds(pl.multiple_of((tp // 2) * 384, 128), 384)
        gate = acc[0]
        hs[s, i, :, columns] = (gate / (1.0 + jnp.exp(-gate)) * acc[1]).astype(BF16)
        h_ring[q].start()

    def out(q):
        s, i = q // 2, q % 2

        def one(n, _):
            columns = pl.ds(pl.multiple_of(n * 256, 256), 256)
            mine = pl.ds(pl.multiple_of(core * 512 + n * 256, 256), 256)
            theirs = pl.ds(pl.multiple_of(512 - core * 512 + n * 256, 256), 256)
            block = hs[s, i]
            swap[s, i, :, columns] = dot(block, down_w[i, :, theirs]).astype(BF16)
            outs[s, 2 * core + i, :, columns] = dot(block, down_w[i, :, mine]).astype(BF16)
            return 0

        lax.fori_loop(0, 2, one, 0)
        c = pltpu.make_async_remote_copy(
            swap.at[s, i],
            outs.at[s, 2 * core + i],
            c_send.at[2 + q],
            c_recv.at[2 + q],
            device_id=mate,
            device_id_type=MESH,
        )
        c.start()
        return c

    def ungroup(s):
        def one(g, _):
            rows = pl.ds(pl.multiple_of(g * BLOCK, 16), BLOCK)
            for h in range(2):
                block = outs[s, :, rows, pl.ds(h * 256, 256)].reshape(ROWS, 256)
                results[s, h, g] = dot(perm[...], block).astype(BF16).reshape(SIDE, BLOCK, 256)
            return 0

        lax.fori_loop(0, SIDE, one, 0)
        give[s].start(0)

    def choose():
        def one(d, _):
            x, z = d // SIDE, lax.rem(d, SIDE)
            home = sel[d]
            for h in range(2):
                chosen[h, x, z] = spread[h, home // SIDE, lax.rem(home, SIDE)]
            return 0

        lax.fori_loop(0, 16, one, 0)
        gather.start(0)

    deal[0].forward()
    deal[1].forward()
    scatter.start(0)
    deal[0].arrive(1)
    swap_x = [regroup(0)]
    swap_x[0].wait()
    x_ring[0].start()
    deal[1].arrive(1)
    swap_x.append(regroup(1))
    swap_x[1].wait()
    x_ring[0].forward()
    x_ring[1].start()
    scatter.forward()
    for mine, theirs in weights:
        mine.wait()
        theirs.wait_recv()
    x_ring[0].arrive()
    hidden(0)
    x_ring[1].forward()
    x_ring[2].start()
    h_ring[0].forward()
    x_ring[1].arrive()
    hidden(1)
    scatter.arrive(1)
    choose()
    x_ring[2].forward()
    x_ring[3].start()
    h_ring[0].arrive()
    swap_o = [out(0)]
    h_ring[1].forward()
    x_ring[2].arrive()
    hidden(2)
    h_ring[1].arrive()
    swap_o.append(out(1))
    swap_o[0].wait()
    swap_o[1].wait()
    ungroup(0)
    x_ring[3].forward()
    gather.forward()
    h_ring[2].forward()
    x_ring[3].arrive()
    hidden(3)
    give[0].forward()
    h_ring[2].arrive()
    swap_o.append(out(2))
    h_ring[3].forward()
    h_ring[3].arrive()
    swap_o.append(out(3))
    swap_o[2].wait()
    swap_o[3].wait()
    ungroup(1)
    give[1].forward()
    gather.arrive(1)
    give[0].arrive(1)
    give[1].arrive(1)
    for one in (*deal, *give, scatter, gather, *x_ring, *h_ring):
        one.sent()
    for _, theirs in weights:
        theirs.wait_send()


def permutation():
    index = np.arange(ROWS).reshape(SIDE, SIDE, CAP).transpose(1, 0, 2).reshape(-1)
    return np.eye(ROWS, dtype=np.float32)[index]


def shards(tokens, expert_ids, route_weight, gate_weight, up_weight, down_weight, home_slot, spare_expert):
    own_index = lax.axis_index("ep")
    experts = lax.iota(jnp.int32, SLOTS)
    spare_slot = jnp.sum(jnp.where(spare_expert[:, None] == experts, home_slot, 0), axis=1)
    spare_home = spare_slot // 4
    own_slot = jnp.max(jnp.where(spare_home == own_index, spare_slot % 4, 0)).reshape(1)
    piece_shape = jax.ShapeDtypeStruct((2, SIDE, SIDE, PIECE, 256), BF16)
    row_shape = jax.ShapeDtypeStruct((STEPS, 2, SIDE, SIDE, BLOCK, 256), BF16)

    outgoing, pieces = pl.pallas_call(
        pack_kernel,
        out_shape=(row_shape, piece_shape),
        in_specs=[SM, VM, VM, VM, ANY, ANY, ANY],
        out_specs=(VM, ANY),
        scratch_shapes=[pltpu.SemaphoreType.DMA((32, 4))],
        compiler_params=pltpu.CompilerParams(vmem_limit_bytes=32 * 2**20),
        name="pack",
    )(own_slot, expert_ids.transpose(0, 2, 1), home_slot.reshape(1, SLOTS), tokens, gate_weight, up_weight, down_weight)

    returned, landed, *_ = pl.pallas_call(
        main_kernel,
        out_shape=(row_shape, piece_shape, piece_shape, piece_shape, row_shape),
        in_specs=[SM, VM, ANY, ANY, ANY, ANY, ANY],
        out_specs=(ANY,) * 5,
        scratch_shapes=[
            pltpu.VMEM((2, 384, 4096), BF16),
            pltpu.VMEM((2, 384, 4096), BF16),
            pltpu.VMEM((2, 1536, 1024), BF16),
            pltpu.VMEM((STEPS, 2, ROWS, 4096), BF16),
            pltpu.VMEM((STEPS, 2, ROWS, 1536), BF16),
            pltpu.VMEM((STEPS, 2, ROWS, 512), BF16),
            pltpu.VMEM((STEPS, 4, ROWS, 512), BF16),
            pltpu.VMEM(row_shape.shape, BF16),
            pltpu.VMEM(row_shape.shape, BF16),
            pltpu.VMEM(row_shape.shape, BF16),
            pltpu.VMEM(piece_shape.shape, BF16),
            pltpu.VMEM(piece_shape.shape, BF16),
            pltpu.VMEM((2, ROWS, 384), F32),
            pltpu.SemaphoreType.DMA((6, 2, 2, 4)),
            pltpu.SemaphoreType.DMA((6, 2, 2, 4)),
            pltpu.SemaphoreType.DMA((4, 4)),
            pltpu.SemaphoreType.DMA((4, 4)),
            pltpu.SemaphoreType.DMA((4, 4)),
            pltpu.SemaphoreType.DMA((4, 4)),
            pltpu.SemaphoreType.DMA((6,)),
            pltpu.SemaphoreType.DMA((6,)),
            pltpu.SemaphoreType.DMA((3,)),
            pltpu.SemaphoreType.DMA((3,)),
            pltpu.SemaphoreType.DMA((3,)),
        ],
        compiler_params=pltpu.CompilerParams(
            collective_id=0, has_side_effects=True, vmem_limit_bytes=60 * 2**20
        ),
        name="exchange",
    )(spare_home, jnp.asarray(permutation(), BF16), outgoing, pieces, gate_weight, up_weight, down_weight)

    return pl.pallas_call(
        mix_kernel,
        out_shape=(
            jax.ShapeDtypeStruct(tokens.shape, BF16),
            jax.ShapeDtypeStruct((1,) + gate_weight.shape[1:], BF16),
            jax.ShapeDtypeStruct((1,) + up_weight.shape[1:], BF16),
            jax.ShapeDtypeStruct((1,) + down_weight.shape[1:], BF16),
        ),
        in_specs=[VM, VM, VM, VM, ANY],
        out_specs=(VM, ANY, ANY, ANY),
        scratch_shapes=[pltpu.SemaphoreType.DMA((32, 4))],
        compiler_params=pltpu.CompilerParams(vmem_limit_bytes=32 * 2**20),
        name="mix",
    )(expert_ids, route_weight, home_slot.reshape(SLOTS, 1), returned, landed)


def solution(mesh):
    placed = (
        P(None, "ep", "tp"),
        P(None, "ep", None),
        P(None, "ep", None),
        P("ep", "tp", None),
        P("ep", "tp", None),
        P("ep", None, "tp"),
        P(),
        P(),
    )
    return jax.shard_map(
        shards,
        mesh=mesh,
        in_specs=placed,
        out_specs=(
            P(None, "ep", "tp"),
            P("ep", "tp", None),
            P("ep", "tp", None),
            P("ep", None, "tp"),
        ),
        check_vma=False,
    )
```

time: 532 us -> 232 us (0.44); the launches traced: 524 us -> 232 us
  Pallas kernels: 0 us -> 213 us
  waiting for transfers between devices: 164 us -> 0 us
  local copies, waits for them, and re-layouts: 124 us -> 15.9 us
  blocking collectives: 72.3 us -> 0 us
  matrix products: 55.7 us -> 0 us
  other arithmetic: 48.5 us -> 2.01 us
  starting transfers between devices: 42.9 us -> 0 us
  between operations: 16.6 us -> 0.71 us
    pallas_call x0 -> x3, Pallas kernels: none -> 213 us  [the longest x1 201 us: shards(): pl.pallas_call(main_kernel, out_shape=(row_shape, piece_shape, piece_shap...]
    all_gather x4 -> x0, waiting for transfers between devices: 132 us -> none  [the longest x2 77.2 us: run_steps(): lax.all_gather(hidden, 'tp', axis=4, tiled=True)]
    all_to_all x3 -> x0, blocking collectives: 72.3 us -> none  [the longest x2 47.6 us: run_steps(): lax.all_to_all(outgoing, 'ep', split_axis=1, concat_axis=1, tiled=True)]
    dot_general x8 -> x0, matrix products: 55.7 us -> none  [the longest x2 22 us: run_steps(): jnp.einsum('bsecd,efd->bsecf', piece_rows, up_weight, preferred_element_t...]
    all_gather x2 -> x0, local copies, waits for them, and re-layouts: 55 us -> none  [run_steps(): lax.all_gather(hidden, 'tp', axis=4, tiled=True)]
    all_to_all x7 -> x0, starting transfers between devices: 42.3 us -> none  [the longest x2 13.8 us: run_steps(): lax.all_to_all(results, 'ep', split_axis=1, concat_axis=1, tiled=True)]
    another operation x4 -> x0, other arithmetic: 36.1 us -> none
    all_to_all x7 -> x0, waiting for transfers between devices: 31.8 us -> none  [the longest x1 17.9 us: move_spares(): lax.all_to_all(chosen_up, 'ep', split_axis=1, concat_axis=1, tiled=True)]
  transfers between devices with their start and end apart: 11 -> 0, of which waited for: 6 -> 0; matrix products, arithmetic and copies ran while one was open for 33% -> 0% of each run, Pallas kernels for 0% -> 0%
where the time goes in v1:
time: 232 us
  Pallas kernels  213 us (92%)
  local copies, waits for them, and re-layouts  15.9 us (7%)
    pallas_call x1, Pallas kernels, shards(): pl.pallas_call(main_kernel, out_shape=(row_shape, piece_shape, piece_shap...  201 us
    unnamed x26, local copies, waits for them, and re-layouts  15.8 us
    pallas_call x1, Pallas kernels, shards(): pl.pallas_call(mix_kernel, out_shape=(jax.ShapeDtypeStruct(tokens.shape,...  6.33 us
    pallas_call x1, Pallas kernels, shards(): pl.pallas_call(pack_kernel, out_shape=(row_shape, piece_shape), in_specs=...  5.81 us

profile of v1, /device:TPU:1, one launch (start us, length us, event | category | flops | bytes accessed | tf_op | source)
XLA Modules:
  0.0 231.9 jit_solution(17410112921079656482)
XLA Ops:
  0.6 0.9 select_reduce_fusion
  1.5 1.2 fusion
  2.6 0.0 copy-start
  2.6 2.8 %copy-done = bf16[4,192,4096]{2,1,0:T(8,128)(2,1)S(1)} copy-done((bf16[4,192,4096]{2,1,0:T(8,128)(2,1)S(1)}, bf16[4,192,4096]{2,1,0:T(8,128)(2,1)}, u32[]{:S(2)}) %copy-start) | copy-done | bytes 6291480
  5.4 0.0 copy-start.1
  5.4 2.8 %copy-done.1 = bf16[4,192,4096]{2,1,0:T(8,128)(2,1)S(1)} copy-done((bf16[4,192,4096]{2,1,0:T(8,128)(2,1)S(1)}, bf16[4,192,4096]{2,1,0:T(8,128)(2,1)}, u32[]{:S(2)}) %copy-start.1) | copy-done | bytes 6291480
  8.2 0.0 copy-start.6
  8.2 0.9 copy-done.6
  9.2 0.0 copy-start.7
  9.2 0.7 copy-done.7
  9.9 0.0 copy-start.9
  9.9 0.7 copy-done.9
  10.5 5.8 %pack.1 = (bf16[2,2,4,4,80,256]{5,4,3,2,1,0:T(8,128)(2,1)S(1)}, bf16[2,4,4,288,256]{4,3,2,1,0:T(8,128)(2,1)S(1)}) custom-call(s32[1]{0:T(128)} %bitcast.1.own_ref, s32[2,8,128]{2,1,0:T(8,128)S(1)} %bitcast.4, s32[1,64]{1,0:T(1,128)S(1)} %bitcast.5, bf16[2,128,512]{2,1,0:T(8,128)(2,1)S(1)} %copy-done.6, bf16[4,192,4096]{2,1,0:T(8,128)(2,1)S(1)} %copy-done, ...), custom_call_target="tpu_custom_call" | custom-call | tf_op jit(solution)/shard_map/pack/pallas_call | solution.py:455
  16.3 0.0 copy-start.2
  16.3 2.1 copy-done.2
  18.5 0.0 copy-start.4
  18.5 1.5 copy-done.4
  20.0 0.0 copy-start.8
  20.0 0.0 copy-start.11
  20.0 0.0 copy-start.10
  20.0 201.1 %exchange.1 = (bf16[2,2,4,4,80,256]{5,4,3,2,1,0:T(8,128)(2,1)}, bf16[2,4,4,288,256]{4,3,2,1,0:T(8,128)(2,1)}, bf16[2,4,4,288,256]{4,3,2,1,0:T(8,128)(2,1)}, bf16...) custom-call(s32[16]{0:T(128)} %get-tuple-element.13.sel, bf16[320,320]{1,0:T(8,128)(2,1)} %constant.39.clone.perm, ...), custom_call_target="tpu_custom_call" | custom-call | tf_op jit(solution)/shard_map/exchange/pallas_call | solution.py:465
  221.1 0.0 copy-done.8
  221.1 0.1 copy.16.ids_ref
  221.2 0.0 copy-done.11
  221.2 0.1 copy.17.rw_ref
  221.4 0.0 copy-done.10
  221.4 0.1 copy.18.home_ref
  221.5 0.0 copy-start.3
  221.5 2.3 %copy-done.3 = bf16[2,4,4,288,256]{4,3,2,1,0:T(8,128)(2,1)S(1)} copy-done((bf16[2,4,4,288,256]{4,3,2,1,0:T(8,128)(2,1)S(1)}, bf16[2,4,4,288,256]{4,3,2,1,0:T(8,128)(2,1)}, u32[]{:S(2)}) %copy-start.3) | copy-done | bytes 4718616
  223.8 0.0 copy-start.5
  223.8 1.7 copy-done.5
  225.5 6.3 %mix.1 = (bf16[2,128,512]{2,1,0:T(8,128)(2,1)}, bf16[1,192,4096]{2,1,0:T(8,128)(2,1)}, bf16[1,192,4096]{2,1,0:T(8,128)(2,1)}, bf16[1,1536,512]{2,1,0:T(8,128)(2,1)}) custom-call(s32[2,128,8]{2,1,0:T(8,128)S(1)} %copy.16.ids_ref, f32[2,128,8]{2,1,0:T(8,128)S(1)} %copy.17.rw_ref, s32[64,1]{1,0:T(8,128)S(1)} %copy.18.home_ref, ...), custom_call_target="tpu_custom_call" | custom-call | tf_op jit(solution)/shard_map/mix/pallas_call | solution.py:502
Async XLA Ops:
  2.6 2.8 %copy-start = (bf16[4,192,4096]{2,1,0:T(8,128)(2,1)S(1)}, bf16[4,192,4096]{2,1,0:T(8,128)(2,1)}, u32[]{:S(2)}) copy-start(bf16[4,192,4096]{2,1,0:T(8,128)(2,1)} %wg.3) | copy-start | bytes 18874372
  5.4 2.8 %copy-start.1 = (bf16[4,192,4096]{2,1,0:T(8,128)(2,1)S(1)}, bf16[4,192,4096]{2,1,0:T(8,128)(2,1)}, u32[]{:S(2)}) copy-start(bf16[4,192,4096]{2,1,0:T(8,128)(2,1)} %wu.3) | copy-start | bytes 18874372
  8.2 0.9 copy-start.6
  9.2 0.7 copy-start.7
  9.9 0.7 copy-start.9
  16.3 2.1 copy-start.2
  18.5 1.5 copy-start.4
  20.0 201.1 %copy-start.8 = (s32[2,128,8]{1,2,0:T(8,128)S(1)}, s32[2,128,8]{1,2,0:T(8,128)}, u32[]{:S(2)}) copy-start(s32[2,128,8]{1,2,0:T(8,128)} %param.10) | copy-start | bytes 24580
  20.0 201.3 %copy-start.11 = (f32[2,128,8]{1,2,0:T(8,128)S(1)}, f32[2,128,8]{1,2,0:T(8,128)}, u32[]{:S(2)}) copy-start(f32[2,128,8]{1,2,0:T(8,128)} %param.11) | copy-start | bytes 24580
  20.0 201.4 %copy-start.10 = (s32[64]{0:T(128)S(1)}, s32[64]{0:T(128)}, u32[]{:S(2)}) copy-start(s32[64]{0:T(128)} %param.15) | copy-start | bytes 772
  221.5 2.3 %copy-start.3 = (bf16[2,4,4,288,256]{4,3,2,1,0:T(8,128)(2,1)S(1)}, bf16[2,4,4,288,256]{4,3,2,1,0:T(8,128)(2,1)}, u32[]{:S(2)}) copy-start(bf16[2,4,4,288,256]{4,3,2,1,0:T(8,128)(2,1)} %get-tuple-element.11.pieces) | copy-start | bytes 14155780
  223.8 1.7 copy-start.5

commit v2 on v1

v2 whole, which is shorter than its diff:
```python
import functools

import jax
import jax.numpy as jnp
import numpy as np
from jax import lax
from jax.experimental import pallas as pl
from jax.experimental.pallas import tpu as pltpu
from jax.sharding import PartitionSpec as P

MESH = pl.DeviceIdType.MESH
BF16 = jnp.bfloat16
F32 = jnp.float32
STEPS = 2
SIDE = 4
CAP = 20
SLOTS = 64
TOK = 128
BLOCK = 4 * CAP
ROWS = 16 * CAP
PAIR = 48
PIECE = 288
HBM = pl.BlockSpec(memory_space=pltpu.MemorySpace.HBM)
VM = pl.BlockSpec(memory_space=pltpu.VMEM)
SM = pl.BlockSpec(memory_space=pltpu.SMEM)


def dot(a, b):
    return jnp.dot(a, b, preferred_element_type=F32)


def dot_t(a, b):
    return lax.dot_general(a, b, (((1,), (1,)), ((), ())), preferred_element_type=F32)


def dot_0(a, b):
    return lax.dot_general(a, b, (((0,), (0,)), ((), ())), preferred_element_type=F32)


def iota(shape, dim):
    return lax.broadcasted_iota(jnp.int32, shape, dim)


def slot_places(ids, home):
    to_slot = (home == iota((SLOTS, SLOTS), 0)).astype(BF16)
    before = (iota((TOK, TOK), 0) < iota((TOK, TOK), 1)).astype(BF16)
    named = iota((SLOTS, TOK), 0)
    picked = jnp.zeros((SLOTS, TOK), F32)
    for k in range(8):
        picked = jnp.where(ids[k : k + 1, :] == named, 1.0, picked)
    by_slot = dot(to_slot, picked.astype(BF16))
    position = dot(by_slot.astype(BF16), before)
    return jnp.where(by_slot > 0.5, position, -1.0).astype(BF16), to_slot


def rows_of(x):
    row = iota((ROWS, SLOTS), 0) + x * ROWS
    low = iota((ROWS, SLOTS), 1) * CAP
    spread = jnp.where((row >= low) & (row < low + CAP), 1.0, 0.0).astype(BF16)
    row = iota((ROWS, TOK), 0) + x * ROWS
    return spread, (row - ((row * 3277) >> 16) * CAP).astype(F32)


def pair_rows_of(x, i):
    def split(width):
        row = iota((SIDE * PAIR, width), 0)
        z = (row * 1366) >> 16
        rest = row - z * PAIR
        c = (rest * 3277) >> 16
        return z, rest, c

    z, rest, c = split(SLOTS)
    slot = (x * SIDE + z) * 4 + 2 * c + i
    spread = jnp.where((slot == iota((SIDE * PAIR, SLOTS), 1)) & (rest < 2 * CAP), 1.0, 0.0).astype(BF16)
    z, rest, c = split(TOK)
    return spread, jnp.where(rest < 2 * CAP, rest - c * CAP, -5).astype(F32)


def mix_kernel(
    ids_ref, rw_ref, home_ref, back_hbm, pair_hbm, pieces, mixed_ref, gate, up, down,
    back, back_pair, held, gate_v, up_v, down_v, in_sem, out_sem,
):
    loads = [pltpu.make_async_copy(pieces.at[h], held.at[h], in_sem.at[h]) for h in range(2)]
    loads.append(pltpu.make_async_copy(back_hbm, back, in_sem.at[2]))
    loads.append(pltpu.make_async_copy(pair_hbm, back_pair, in_sem.at[3]))
    for c in loads:
        c.start()
    writes = []
    for h in range(2):
        loads[h].wait()

        def one(p, _, h=h):
            of = held.at[h, p // SIDE, lax.rem(p, SIDE)]
            columns = pl.ds(pl.multiple_of(p * 256, 256), 256)
            low = pl.ds(pl.multiple_of(h * 768 + p * 48, 16), 48)
            gate_v[pl.ds(h * 96, 96), columns] = of[pl.ds(0, 96)]
            up_v[pl.ds(h * 96, 96), columns] = of[pl.ds(96, 96)]
            down_v[low, pl.ds(0, 256)] = of[pl.ds(192, 48)]
            down_v[low, pl.ds(256, 256)] = of[pl.ds(240, 48)]
            return 0

        lax.fori_loop(0, 16, one, 0)
        for n, (a, b, rows) in enumerate(((gate_v, gate, 96), (up_v, up, 96), (down_v, down, 768))):
            part = pl.ds(h * rows, rows)
            writes.append(pltpu.make_async_copy(a.at[part], b.at[0, part], out_sem.at[h, n]))
            writes[-1].start()
    loads[2].wait()
    loads[3].wait()
    for s in range(STEPS):
        places, to_slot = slot_places(ids_ref[s], home_ref[...])
        named = iota((SLOTS, TOK), 0)
        scale = jnp.zeros((SLOTS, TOK), F32)
        for k in range(8):
            scale = jnp.where(ids_ref[s, k : k + 1, :] == named, rw_ref[s, k : k + 1, :], scale)
        high = scale.astype(BF16)
        rest = (scale - high.astype(F32)).astype(BF16)
        high = dot(to_slot, high).astype(BF16)
        rest = dot(to_slot, rest).astype(BF16)
        totals = [jnp.zeros((TOK, 256), F32)] * 2
        parts = [(x, i) for x in range(SIDE) for i in range(2 if s else 1)]
        for x, i in parts:
            spread, within = pair_rows_of(x, i) if s else rows_of(x)
            here = dot(spread, places) == within
            high_row = jnp.where(here, dot(spread, high), 0.0).astype(BF16)
            rest_row = jnp.where(here, dot(spread, rest), 0.0).astype(BF16)
            for h in range(2):
                block = back_pair[i, h, x].reshape(SIDE * PAIR, 256) if s else back[h, x].reshape(ROWS, 256)
                totals[h] = totals[h] + dot_0(high_row, block) + dot_0(rest_row, block)
        for h in range(2):
            mixed_ref[s, :, h * 256 : (h + 1) * 256] = totals[h].astype(BF16)

    for c in writes:
        c.wait()


class Exchange:
    def __init__(self, number, src, mid, dst, send, recv):
        ep, tp = lax.axis_index("ep"), lax.axis_index("tp")
        self.ex, self.ez, self.tp = ep // SIDE, lax.rem(ep, SIDE), tp
        self.src, self.mid, self.dst = src, mid, dst
        self.send, self.recv, self.number = send, recv, number
        self.started = []

    def copy(self, phase, half, d):
        ex, ez = self.ex, self.ez
        along_x = half == phase
        x = lax.rem(ex + d, SIDE) if along_x else ex
        z = ez if along_x else lax.rem(ez + d, SIDE)
        if phase == 0:
            a = self.src.at[0, x] if half == 0 else self.src.at[1, :, z]
            b = self.mid.at[half, ex if half == 0 else ez]
        else:
            a = self.mid.at[half, :, z if half == 0 else x]
            b = self.dst.at[0, :, ez] if half == 0 else self.dst.at[1, ex]
        send = self.send.at[self.number, phase, half, d]
        if d == 0:
            return pltpu.make_async_copy(a, b, send)
        recv = self.recv.at[self.number, phase, half, d]
        return pltpu.make_async_remote_copy(
            a, b, send, recv, device_id=(x * SIDE + z, self.tp), device_id_type=MESH
        )

    def start(self, phase):
        for d in (2, 1, 3, 0):
            for half in range(2):
                c = self.copy(phase, half, d)
                c.start()
                self.started.append((phase, d, c))

    def arrive(self, phase):
        for at, d, c in self.started:
            if at == phase:
                c.wait() if d == 0 else c.wait_recv()

    def forward(self):
        self.arrive(0)
        self.start(1)

    def sent(self):
        for _, d, c in self.started:
            if d:
                c.wait_send()


class Ring:
    def __init__(self, number, ref, width, send, recv):
        self.ep, self.tp = lax.axis_index("ep"), lax.axis_index("tp")
        self.y = self.tp // 2
        self.ref, self.width, self.number = ref, width, number
        self.send, self.recv = send, recv
        self.all = {}

    def copy(self, kind):
        y = lax.rem(self.y + (0, 0, 3, 1)[kind], 4)
        to = lax.rem(self.tp + (2, 6, 2, 6)[kind], 8)
        rows = (pl.ds(0, ROWS), pl.ds(0, ROWS), pl.ds(0, ROWS // 2), pl.ds(ROWS // 2, ROWS // 2))[kind]
        part = self.ref.at[rows, pl.ds(pl.multiple_of(y * self.width, 128), self.width)]
        return pltpu.make_async_remote_copy(
            part,
            part,
            self.send.at[self.number, kind],
            self.recv.at[self.number, kind],
            device_id=(self.ep, to),
            device_id_type=MESH,
        )

    def start(self):
        for kind in (0, 1):
            self.all[kind] = self.copy(kind)
            self.all[kind].start()

    def forward(self):
        for kind in (0, 1):
            self.all[kind].wait_recv()
            self.all[kind + 2] = self.copy(kind + 2)
            self.all[kind + 2].start()

    def arrive(self):
        for kind in (2, 3):
            self.all[kind].wait_recv()

    def sent(self):
        for c in self.all.values():
            c.wait_send()


def main_kernel(
    home_s, spare_s, home_ref, ids_ref, tok_ref, perm, pair_perm, wg, wu, wd,
    returned, returned_pair, landed, mid_a,
    gate_w, up_w, down_w, xs, hs, swap, outs, arrived, outgoing, mid_d, mid_r, out_pair, mid_pair, spread, chosen, acc,
    a_send, a_recv, x_send, x_recv, h_send, h_recv, c_send, c_recv, w_send, w_recv, w_local, p_local, credit,
):
    ep, tp = lax.axis_index("ep"), lax.axis_index("tp")
    ex, ez = ep // SIDE, lax.rem(ep, SIDE)
    core = lax.rem(tp, 2)
    mate = (ep, tp + 1 - 2 * core)

    barrier = pltpu.get_barrier_semaphore()
    for d in range(1, SIDE):
        pl.semaphore_signal(barrier, inc=1, device_id=(lax.rem(ex + d, SIDE) * SIDE + ez, tp), device_id_type=MESH)
        pl.semaphore_signal(barrier, inc=1, device_id=(ex * SIDE + lax.rem(ez + d, SIDE), tp), device_id_type=MESH)
    pl.semaphore_signal(barrier, inc=1, device_id=(ep, lax.rem(tp + 2, 8)), device_id_type=MESH)
    pl.semaphore_signal(barrier, inc=1, device_id=(ep, lax.rem(tp + 6, 8)), device_id_type=MESH)
    pl.semaphore_signal(barrier, inc=1, device_id=mate, device_id_type=MESH)

    deal = [Exchange(s, outgoing.at[s], mid_d.at[s], arrived.at[s], a_send, a_recv) for s in range(STEPS)]
    give = [Exchange(2, outgoing.at[0], mid_r, returned, a_send, a_recv)]
    for i in range(2):
        give.append(Exchange(3 + i, out_pair.at[i], mid_pair.at[i], returned_pair.at[i], a_send, a_recv))
    scatter = Exchange(5, chosen, mid_a, spread, a_send, a_recv)
    gather = Exchange(6, chosen, spread, landed, a_send, a_recv)
    x_ring = [Ring(q, xs.at[q], 1024, x_send, x_recv) for q in range(4)]
    h_ring = [Ring(q, hs.at[q], 384, h_send, h_recv) for q in range(4)]

    own_two, mate_two = pl.ds(2 * core, 2), pl.ds(2 - 2 * core, 2)
    own_rows = pl.ds(pl.multiple_of(core * 192, 16), 192)
    own_half = pl.ds(pl.multiple_of(core * 512, 512), 512)
    mate_half = pl.ds(pl.multiple_of(512 - core * 512, 512), 512)
    weights = []
    for n, (w, held) in enumerate(((wg, gate_w), (wu, up_w), (wd, down_w))):
        to = held.at[:, :, own_half] if n == 2 else held.at[:, own_rows]
        mine = pltpu.make_async_copy(w.at[own_two], to, w_local.at[n])
        theirs = pltpu.make_async_remote_copy(
            w.at[mate_two], to, w_send.at[n], w_recv.at[n], device_id=mate, device_id_type=MESH
        )
        weights.append((mine, theirs))

    own_perm = pl.ds(pl.multiple_of(core * 160, 16), 160)
    mate_perm = pl.ds(pl.multiple_of(160 - core * 160, 16), 160)

    def regroup(s):
        def one(g, _):
            rows = pl.ds(pl.multiple_of(g * BLOCK, 16), BLOCK)
            for h in range(2):
                block = arrived[s, h, g].reshape(ROWS, 256)
                mine = dot(perm[own_perm, :], block).astype(BF16)
                theirs = dot(perm[mate_perm, :], block).astype(BF16)
                columns = pl.ds(pl.multiple_of(tp * 512 + h * 256, 256), 256)
                for i in range(2):
                    xs[2 * s + i, rows, columns] = mine[i * BLOCK : (i + 1) * BLOCK]
                    swap[s, i, rows, pl.ds(h * 256, 256)] = theirs[i * BLOCK : (i + 1) * BLOCK]
            return 0

        lax.fori_loop(0, SIDE, one, 0)
        c = pltpu.make_async_remote_copy(
            swap.at[s],
            xs.at[pl.ds(2 * s, 2), :, pl.ds(pl.multiple_of(tp * 512, 512), 512)],
            c_send.at[s],
            c_recv.at[s],
            device_id=mate,
            device_id_type=MESH,
        )
        c.start()
        return c

    def hidden(q):
        i = q % 2
        acc[...] = jnp.zeros_like(acc)

        def one(k, _):
            columns = pl.ds(pl.multiple_of(k * 512, 512), 512)
            block = xs[q, :, columns]
            acc[0] += dot_t(block, gate_w[i, :, columns])
            acc[1] += dot_t(block, up_w[i, :, columns])
            return 0

        lax.fori_loop(0, 8, one, 0)
        columns = pl.ds(pl.multiple_of((tp // 2) * 384, 128), 384)
        gate = acc[0]
        hs[q, :, columns] = (gate / (1.0 + jnp.exp(-gate)) * acc[1]).astype(BF16)
        h_ring[q].start()

    def out(q):
        s, i = q // 2, q % 2

        def one(n, _):
            columns = pl.ds(pl.multiple_of(n * 256, 256), 256)
            mine = pl.ds(pl.multiple_of(core * 512 + n * 256, 256), 256)
            theirs = pl.ds(pl.multiple_of(512 - core * 512 + n * 256, 256), 256)
            block = hs[q]
            swap[s, i, :, columns] = dot(block, down_w[i, :, theirs]).astype(BF16)
            outs[s, 2 * core + i, :, columns] = dot(block, down_w[i, :, mine]).astype(BF16)
            return 0

        lax.fori_loop(0, 2, one, 0)
        c = pltpu.make_async_remote_copy(
            swap.at[s, i],
            outs.at[s, 2 * core + i],
            c_send.at[2 + q],
            c_recv.at[2 + q],
            device_id=mate,
            device_id_type=MESH,
        )
        c.start()
        return c

    def ungroup():
        def one(g, _):
            rows = pl.ds(pl.multiple_of(g * BLOCK, 16), BLOCK)
            for h in range(2):
                block = outs[0, :, rows, pl.ds(h * 256, 256)].reshape(ROWS, 256)
                outgoing[0, h, g] = dot(perm[...], block).astype(BF16).reshape(SIDE, BLOCK, 256)
            return 0

        lax.fori_loop(0, SIDE, one, 0)
        give[0].start(0)

    def ungroup_pair(i):
        def one(g, _):
            rows = pl.ds(pl.multiple_of(g * BLOCK, 16), BLOCK)
            for h in range(2):
                columns = pl.ds(h * 256, 256)
                total = dot(pair_perm[0], outs[1, i, rows, columns]) + dot(pair_perm[1], outs[1, 2 + i, rows, columns])
                out_pair[i, h, g] = total.astype(BF16).reshape(SIDE, PAIR, 256)
            return 0

        lax.fori_loop(0, SIDE, one, 0)
        give[1 + i].start(0)

    def choose():
        def one(d, _):
            x, z = d // SIDE, lax.rem(d, SIDE)
            home = home_s[spare_s[d]] // 4
            for h in range(2):
                chosen[h, x, z] = spread[h, home // SIDE, lax.rem(home, SIDE)]
            return 0

        lax.fori_loop(0, 16, one, 0)
        for d in range(1, SIDE):
            along_x, along_z = lax.rem(ex + d, SIDE) * SIDE + ez, ex * SIDE + lax.rem(ez + d, SIDE)
            pl.semaphore_signal(credit, inc=1, device_id=(along_x, tp), device_id_type=MESH)
            pl.semaphore_signal(credit, inc=1, device_id=(along_z, tp), device_id_type=MESH)
        pl.semaphore_wait(credit, 6)
        gather.start(0)

    def place(s):
        places, _ = slot_places(ids_ref[s], home_ref[...])

        def one(x, _):
            spread_rows, within = rows_of(x)
            placing = jnp.where(dot(spread_rows, places) == within, 1.0, 0.0).astype(BF16)
            for h in range(2):
                block = dot(placing, tok_ref[s, :, h * 256 : (h + 1) * 256]).astype(BF16)
                outgoing[s, h, x] = block.reshape(SIDE, BLOCK, 256)
            return 0

        lax.fori_loop(0, SIDE, one, 0)

    def fetch(j):
        h, two, b = j // 8, lax.rem(j, 8), lax.rem(j, 3)
        rows = pl.ds(pl.multiple_of(h * 96, 16), 96)
        columns = pl.ds(pl.multiple_of(two * 512, 512), 512)
        low = pl.ds(pl.multiple_of(h * 768 + two * 96, 16), 96)
        to = pl.ds(pl.multiple_of(b * 96, 16), 96)
        return [
            pltpu.make_async_copy(wg.at[:, rows, columns], hs.at[:, to, pl.ds(0, 512)], p_local.at[b, 0]),
            pltpu.make_async_copy(wu.at[:, rows, columns], hs.at[:, to, pl.ds(512, 512)], p_local.at[b, 1]),
            pltpu.make_async_copy(wd.at[:, low, :], hs.at[:, to, pl.ds(1024, 512)], p_local.at[b, 2]),
        ]

    def fetch_start(j):
        for c in fetch(j):
            c.start()

    def cut():
        def find(d, own):
            slot = home_s[spare_s[d]]
            return jnp.maximum(own, jnp.where(slot // 4 == ep, lax.rem(slot, 4), 0))

        own = lax.fori_loop(0, 16, find, jnp.int32(0))

        def one(j, _):
            for c in fetch(j):
                c.wait()
            h, two, b = j // 8, lax.rem(j, 8), lax.rem(j, 3)
            px, pair = two // 2, lax.rem(two, 2)

            def pick(low, rows, columns):
                at = pl.ds(pl.multiple_of(b * 96 + low, 16), rows)
                value = hs[0, at, columns]
                for k in range(1, 4):
                    value = jnp.where(own == k, hs[k, at, columns], value)
                return value

            for z in range(2):
                to = chosen.at[h, px, 2 * pair + z]
                for n in range(2):
                    to[pl.ds(96 * n, 96)] = pick(0, 96, pl.ds(512 * n + 256 * z, 256))
                    to[pl.ds(192 + 48 * n, 48)] = pick(48 * z, 48, pl.ds(1024 + 256 * n, 256))
            return 0

        def more(j, _):
            one(j, 0)
            fetch_start(j + 3)
            return 0

        lax.fori_loop(0, 13, more, 0)
        lax.fori_loop(13, 16, one, 0)

    for j in range(3):
        fetch_start(j)
    place(0)
    pl.semaphore_wait(barrier, 9)
    deal[0].start(0)
    for mine, theirs in weights:
        theirs.start()
        mine.start()
    deal[0].forward()
    place(1)
    deal[0].arrive(1)
    swap_x = [regroup(0)]
    deal[1].start(0)
    swap_x[0].wait()
    x_ring[0].start()
    cut()
    deal[1].forward()
    scatter.start(0)
    x_ring[0].forward()
    x_ring[1].start()
    for mine, theirs in weights:
        mine.wait()
        theirs.wait_recv()
    x_ring[0].arrive()
    hidden(0)
    deal[1].arrive(1)
    swap_x.append(regroup(1))
    swap_x[1].wait()
    x_ring[1].forward()
    x_ring[2].start()
    h_ring[0].forward()
    scatter.forward()
    x_ring[1].arrive()
    hidden(1)
    h_ring[0].arrive()
    swap_o = [out(0)]
    x_ring[2].forward()
    x_ring[3].start()
    h_ring[1].forward()
    scatter.arrive(1)
    scatter.sent()
    choose()
    x_ring[2].arrive()
    hidden(2)
    h_ring[1].arrive()
    swap_o.append(out(1))
    swap_o[0].wait()
    swap_o[1].wait()
    for one in deal:
        one.sent()
    ungroup()
    x_ring[3].forward()
    h_ring[2].forward()
    gather.forward()
    x_ring[3].arrive()
    hidden(3)
    give[0].forward()
    h_ring[2].arrive()
    swap_o.append(out(2))
    swap_o[2].wait()
    ungroup_pair(0)
    h_ring[3].forward()
    h_ring[3].arrive()
    swap_o.append(out(3))
    swap_o[3].wait()
    ungroup_pair(1)
    give[1].forward()
    give[2].forward()
    gather.arrive(1)
    for one in give:
        one.arrive(1)
    for one in (*give, gather, *x_ring, *h_ring):
        one.sent()
    for _, theirs in weights:
        theirs.wait_send()


def permutation():
    index = np.arange(ROWS).reshape(SIDE, SIDE, CAP).transpose(1, 0, 2).reshape(-1)
    return np.eye(ROWS, dtype=np.float32)[index]


def pair_permutations():
    out = np.zeros((2, SIDE * PAIR, BLOCK), np.float32)
    for c in range(2):
        for z in range(SIDE):
            out[c, z * PAIR + c * CAP + np.arange(CAP), z * CAP + np.arange(CAP)] = 1.0
    return out


def shards(tokens, expert_ids, route_weight, gate_weight, up_weight, down_weight, home_slot, spare_expert):
    ids = expert_ids.transpose(0, 2, 1)
    home_row = home_slot.reshape(1, SLOTS)
    piece_shape = jax.ShapeDtypeStruct((2, SIDE, SIDE, PIECE, 256), BF16)
    row_shape = jax.ShapeDtypeStruct((STEPS, 2, SIDE, SIDE, BLOCK, 256), BF16)
    one_shape = jax.ShapeDtypeStruct((2, SIDE, SIDE, BLOCK, 256), BF16)
    pair_shape = jax.ShapeDtypeStruct((2, 2, SIDE, SIDE, PAIR, 256), BF16)

    returned, returned_pair, landed, *_ = pl.pallas_call(
        main_kernel,
        out_shape=(one_shape, pair_shape, piece_shape, piece_shape),
        in_specs=[SM, SM, VM, VM, VM, VM, VM, HBM, HBM, HBM],
        out_specs=(HBM,) * 4,
        scratch_shapes=[
            pltpu.VMEM((2, 384, 4096), BF16),
            pltpu.VMEM((2, 384, 4096), BF16),
            pltpu.VMEM((2, 1536, 1024), BF16),
            pltpu.VMEM((4, ROWS, 4096), BF16),
            pltpu.VMEM((4, ROWS, 1536), BF16),
            pltpu.VMEM((STEPS, 2, ROWS, 512), BF16),
            pltpu.VMEM((STEPS, 4, ROWS, 512), BF16),
            pltpu.VMEM(row_shape.shape, BF16),
            pltpu.VMEM(row_shape.shape, BF16),
            pltpu.VMEM(row_shape.shape, BF16),
            pltpu.VMEM(one_shape.shape, BF16),
            pltpu.VMEM(pair_shape.shape, BF16),
            pltpu.VMEM(pair_shape.shape, BF16),
            pltpu.VMEM(piece_shape.shape, BF16),
            pltpu.VMEM(piece_shape.shape, BF16),
            pltpu.VMEM((2, ROWS, 384), F32),
            pltpu.SemaphoreType.DMA((7, 2, 2, 4)),
            pltpu.SemaphoreType.DMA((7, 2, 2, 4)),
            pltpu.SemaphoreType.DMA((4, 4)),
            pltpu.SemaphoreType.DMA((4, 4)),
            pltpu.SemaphoreType.DMA((4, 4)),
            pltpu.SemaphoreType.DMA((4, 4)),
            pltpu.SemaphoreType.DMA((6,)),
            pltpu.SemaphoreType.DMA((6,)),
            pltpu.SemaphoreType.DMA((3,)),
            pltpu.SemaphoreType.DMA((3,)),
            pltpu.SemaphoreType.DMA((3,)),
            pltpu.SemaphoreType.DMA((3, 3)),
            pltpu.SemaphoreType.REGULAR,
        ],
        compiler_params=pltpu.CompilerParams(
            collective_id=0, has_side_effects=True, vmem_limit_bytes=60 * 2**20
        ),
        name="exchange",
    )(
        home_slot,
        spare_expert,
        home_row,
        ids,
        tokens,
        jnp.asarray(permutation(), BF16),
        jnp.asarray(pair_permutations(), BF16),
        gate_weight,
        up_weight,
        down_weight,
    )

    return pl.pallas_call(
        mix_kernel,
        out_shape=(
            jax.ShapeDtypeStruct(tokens.shape, BF16),
            jax.ShapeDtypeStruct((1,) + gate_weight.shape[1:], BF16),
            jax.ShapeDtypeStruct((1,) + up_weight.shape[1:], BF16),
            jax.ShapeDtypeStruct((1,) + down_weight.shape[1:], BF16),
        ),
        in_specs=[VM, VM, VM, HBM, HBM, HBM],
        out_specs=(VM, HBM, HBM, HBM),
        scratch_shapes=[
            pltpu.VMEM(one_shape.shape, BF16),
            pltpu.VMEM(pair_shape.shape, BF16),
            pltpu.VMEM(piece_shape.shape, BF16),
            pltpu.VMEM(gate_weight.shape[1:], BF16),
            pltpu.VMEM(up_weight.shape[1:], BF16),
            pltpu.VMEM(down_weight.shape[1:], BF16),
            pltpu.SemaphoreType.DMA((4,)),
            pltpu.SemaphoreType.DMA((2, 3)),
        ],
        compiler_params=pltpu.CompilerParams(vmem_limit_bytes=60 * 2**20),
        name="mix",
    )(ids, route_weight.transpose(0, 2, 1), home_row, returned, returned_pair, landed)


def solution(mesh):
    placed = (
        P(None, "ep", "tp"),
        P(None, "ep", None),
        P(None, "ep", None),
        P("ep", "tp", None),
        P("ep", "tp", None),
        P("ep", None, "tp"),
        P(),
        P(),
    )
    return jax.shard_map(
        shards,
        mesh=mesh,
        in_specs=placed,
        out_specs=(
            P(None, "ep", "tp"),
            P("ep", "tp", None),
            P("ep", "tp", None),
            P("ep", None, "tp"),
        ),
        check_vma=False,
    )
```

time: 232 us -> 206 us (0.89)
  local copies, waits for them, and re-layouts: 15.9 us -> 0 us
  Pallas kernels: 213 us -> 205 us
    unnamed x26 -> x0, local copies, waits for them, and re-layouts: 15.8 us -> none
    pallas_call x2 -> x1, Pallas kernels: 207 us -> 195 us  [shards(): pl.pallas_call(main_kernel, out_shape=(one_shape, pair_shape, piece_shape...]
    pallas_call x1, Pallas kernels: 6.33 us -> 9.86 us  [shards(): pl.pallas_call(mix_kernel, out_shape=(jax.ShapeDtypeStruct(tokens.shape,...]
where the time goes in v2:
time: 206 us
  Pallas kernels  205 us (100%)
    pallas_call x1, Pallas kernels, shards(): pl.pallas_call(main_kernel, out_shape=(one_shape, pair_shape, piece_shape...  195 us
    pallas_call x1, Pallas kernels, shards(): pl.pallas_call(mix_kernel, out_shape=(jax.ShapeDtypeStruct(tokens.shape,...  9.86 us

profile of v2, /device:TPU:1, one launch (start us, length us, event | category | flops | bytes accessed | tf_op | source)
XLA Modules:
  0.0 205.6 jit_solution(17663175995188649994)
XLA Ops:
  0.6 195.1 %exchange.1 = (bf16[2,4,4,80,256]{4,3,2,1,0:T(8,128)(2,1)}, bf16[2,2,4,4,48,256]{5,4,3,2,1,0:T(8,128)(2,1)}, bf16[2,4,4,288,256]{4,3,2,1,0:T(8,128)(2,1)}, bf16[2,4,4,288,256]{4,3,2,1,0:T(8,128)(2,1)}) custom-call(s32[64]{0:T(128)} %home_s.1, s32[16]{0:T(128)} %spare_s.1, s32[1,64]{1,0:T(1,128)} %bitcast.6, s32[2,8,128]{2,1,0:T(8,128)} %bitcast.3, ...), custom_call_target="tpu_custom_call" | custom-call | tf_op jit(solution)/shard_map/exchange/pallas_call | solution.py:538
  195.8 9.9 %mix.1 = (bf16[2,128,512]{2,1,0:T(8,128)(2,1)}, bf16[1,192,4096]{2,1,0:T(8,128)(2,1)}, bf16[1,192,4096]{2,1,0:T(8,128)(2,1)}, bf16[1,1536,512]{2,1,0:T(8,128)(2,1)}) custom-call(s32[2,8,128]{2,1,0:T(8,128)} %bitcast.4, f32[2,8,128]{2,1,0:T(8,128)} %bitcast.5, s32[1,64]{1,0:T(1,128)} %bitcast.7, bf16[2,4,4,80,256]{4,3,2,1,0:T(8,128)(2,1)} %get-tuple-element.7.back_hbm, ...), custom_call_target="tpu_custom_call" | custom-call | tf_op jit(solution)/shard_map/mix/pallas_call | solution.py:591

commit v3 on v2

--- a/solution.py
+++ b/solution.py
@@ -80,16 +80,19 @@
     ids_ref, rw_ref, home_ref, back_hbm, pair_hbm, pieces, mixed_ref, gate, up, down,
     back, back_pair, held, gate_v, up_v, down_v, in_sem, out_sem,
 ):
-    loads = [pltpu.make_async_copy(pieces.at[h], held.at[h], in_sem.at[h]) for h in range(2)]
-    loads.append(pltpu.make_async_copy(back_hbm, back, in_sem.at[2]))
-    loads.append(pltpu.make_async_copy(pair_hbm, back_pair, in_sem.at[3]))
+    loads = [
+        pltpu.make_async_copy(back_hbm, back, in_sem.at[0]),
+        pltpu.make_async_copy(pair_hbm, back_pair, in_sem.at[1]),
+    ]
+    loads += [pltpu.make_async_copy(pieces.at[h], held.at[h], in_sem.at[2 + h]) for h in range(2)]
     for c in loads:
         c.start()
     writes = []
-    for h in range(2):
-        loads[h].wait()
-
-        def one(p, _, h=h):
+
+    def join(h):
+        loads[2 + h].wait()
+
+        def one(p, _):
             of = held.at[h, p // SIDE, lax.rem(p, SIDE)]
             columns = pl.ds(pl.multiple_of(p * 256, 256), 256)
             low = pl.ds(pl.multiple_of(h * 768 + p * 48, 16), 48)
@@ -104,9 +107,8 @@
             part = pl.ds(h * rows, rows)
             writes.append(pltpu.make_async_copy(a.at[part], b.at[0, part], out_sem.at[h, n]))
             writes[-1].start()
-    loads[2].wait()
-    loads[3].wait()
-    for s in range(STEPS):
+
+    def mix(s):
         places, to_slot = slot_places(ids_ref[s], home_ref[...])
         named = iota((SLOTS, TOK), 0)
         scale = jnp.zeros((SLOTS, TOK), F32)
@@ -117,6 +119,7 @@
         high = dot(to_slot, high).astype(BF16)
         rest = dot(to_slot, rest).astype(BF16)
         totals = [jnp.zeros((TOK, 256), F32)] * 2
+        loads[s].wait()
         parts = [(x, i) for x in range(SIDE) for i in range(2 if s else 1)]
         for x, i in parts:
             spread, within = pair_rows_of(x, i) if s else rows_of(x)
@@ -129,6 +132,10 @@
         for h in range(2):
             mixed_ref[s, :, h * 256 : (h + 1) * 256] = totals[h].astype(BF16)
 
+    mix(0)
+    join(0)
+    join(1)
+    mix(1)
     for c in writes:
         c.wait()
 
@@ -402,7 +409,7 @@
         for c in fetch(j):
             c.start()
 
-    def cut():
+    def cut(first, end):
         def find(d, own):
             slot = home_s[spare_s[d]]
             return jnp.maximum(own, jnp.where(slot // 4 == ep, lax.rem(slot, 4), 0))
@@ -434,8 +441,9 @@
             fetch_start(j + 3)
             return 0
 
-        lax.fori_loop(0, 13, more, 0)
-        lax.fori_loop(13, 16, one, 0)
+        lax.fori_loop(first, min(end, 13), more, 0)
+        if end == 16:
+            lax.fori_loop(13, 16, one, 0)
 
     for j in range(3):
         fetch_start(j)
@@ -452,8 +460,9 @@
     deal[1].start(0)
     swap_x[0].wait()
     x_ring[0].start()
-    cut()
+    cut(0, 8)
     deal[1].forward()
+    cut(8, 16)
     scatter.start(0)
     x_ring[0].forward()
     x_ring[1].start()

time: 206 us -> 204 us (level)
  no operation moved by 1% of the time
where the time goes in v3:
time: 204 us
  Pallas kernels  203 us (100%)
    pallas_call x1, Pallas kernels, shards(): pl.pallas_call(main_kernel, out_shape=(one_shape, pair_shape, piece_shape...  195 us
    pallas_call x1, Pallas kernels, shards(): pl.pallas_call(mix_kernel, out_shape=(jax.ShapeDtypeStruct(tokens.shape,...  7.88 us

profile of v3, /device:TPU:1, one launch (start us, length us, event | category | flops | bytes accessed | tf_op | source)
XLA Modules:
  0.0 203.7 jit_solution(433685009164911906)
XLA Ops:
  0.6 195.1 %exchange.1 = (bf16[2,4,4,80,256]{4,3,2,1,0:T(8,128)(2,1)}, bf16[2,2,4,4,48,256]{5,4,3,2,1,0:T(8,128)(2,1)}, bf16[2,4,4,288,256]{4,3,2,1,0:T(8,128)(2,1)}, bf16[2,4,4,288,256]{4,3,2,1,0:T(8,128)(2,1)}) custom-call(s32[64]{0:T(128)} %home_s.1, s32[16]{0:T(128)} %spare_s.1, s32[1,64]{1,0:T(1,128)} %bitcast.6, s32[2,8,128]{2,1,0:T(8,128)} %bitcast.3, ...), custom_call_target="tpu_custom_call" | custom-call | tf_op jit(solution)/shard_map/exchange/pallas_call | solution.py:547
  195.8 7.9 %mix.1 = (bf16[2,128,512]{2,1,0:T(8,128)(2,1)}, bf16[1,192,4096]{2,1,0:T(8,128)(2,1)}, bf16[1,192,4096]{2,1,0:T(8,128)(2,1)}, bf16[1,1536,512]{2,1,0:T(8,128)(2,1)}) custom-call(s32[2,8,128]{2,1,0:T(8,128)} %bitcast.4, f32[2,8,128]{2,1,0:T(8,128)} %bitcast.5, s32[1,64]{1,0:T(1,128)} %bitcast.7, bf16[2,4,4,80,256]{4,3,2,1,0:T(8,128)(2,1)} %get-tuple-element.7.back_hbm, ...), custom_call_target="tpu_custom_call" | custom-call | tf_op jit(solution)/shard_map/mix/pallas_call | solution.py:600

commit v4 on v3

--- a/solution.py
+++ b/solution.py
@@ -168,7 +168,7 @@
         )
 
     def start(self, phase):
-        for d in (2, 1, 3, 0):
+        for d in (1, 3, 2, 0):
             for half in range(2):
                 c = self.copy(phase, half, d)
                 c.start()

time: 204 us -> 203 us (level)
  no operation moved by 1% of the time
where the time goes in v4:
time: 203 us
  Pallas kernels  202 us (100%)
    pallas_call x1, Pallas kernels, shards(): pl.pallas_call(main_kernel, out_shape=(one_shape, pair_shape, piece_shape...  194 us
    pallas_call x1, Pallas kernels, shards(): pl.pallas_call(mix_kernel, out_shape=(jax.ShapeDtypeStruct(tokens.shape,...  7.87 us

profile of v4, /device:TPU:1, one launch (start us, length us, event | category | flops | bytes accessed | tf_op | source)
XLA Modules:
  0.0 203.0 jit_solution(10901886793492233391)
XLA Ops:
  0.6 194.5 %exchange.1 = (bf16[2,4,4,80,256]{4,3,2,1,0:T(8,128)(2,1)}, bf16[2,2,4,4,48,256]{5,4,3,2,1,0:T(8,128)(2,1)}, bf16[2,4,4,288,256]{4,3,2,1,0:T(8,128)(2,1)}, bf16[2,4,4,288,256]{4,3,2,1,0:T(8,128)(2,1)}) custom-call(s32[64]{0:T(128)} %home_s.1, s32[16]{0:T(128)} %spare_s.1, s32[1,64]{1,0:T(1,128)} %bitcast.6, s32[2,8,128]{2,1,0:T(8,128)} %bitcast.3, ...), custom_call_target="tpu_custom_call" | custom-call | tf_op jit(solution)/shard_map/exchange/pallas_call | solution.py:547
  195.1 7.9 %mix.1 = (bf16[2,128,512]{2,1,0:T(8,128)(2,1)}, bf16[1,192,4096]{2,1,0:T(8,128)(2,1)}, bf16[1,192,4096]{2,1,0:T(8,128)(2,1)}, bf16[1,1536,512]{2,1,0:T(8,128)(2,1)}) custom-call(s32[2,8,128]{2,1,0:T(8,128)} %bitcast.4, f32[2,8,128]{2,1,0:T(8,128)} %bitcast.5, s32[1,64]{1,0:T(1,128)} %bitcast.7, bf16[2,4,4,80,256]{4,3,2,1,0:T(8,128)(2,1)} %get-tuple-element.7.back_hbm, ...), custom_call_target="tpu_custom_call" | custom-call | tf_op jit(solution)/shard_map/mix/pallas_call | solution.py:600
